TPU v7x, 256 devices: a whole 4x4x8 slice. The times are simulated.
256 devices in a mesh: fsdp: 64 (over z, x_hi, y), tensor: 4 (over x_lo, core).
Axes of the slice: x: 4 (x_hi: 2, x_lo: 2; x = x_hi * 2 + x_lo), y: 4, z: 8, core: 2. Of those that a mesh axis runs over, the one named last changes fastest.
Arguments:
- head_out: bfloat16 [32768, 3072], P('fsdp', 'tensor'), may hold values from -6 to 6
- stream: bfloat16 [32768, 4608], P('fsdp', 'tensor'), may hold values from -100 to 100
- tangent: bfloat16 [4608, 3072], P('fsdp', 'tensor'), may hold values from -2 to 2
- norm_gain: bfloat16 [4608], P('tensor'), may hold values from 0.099609375 to 1.8984375
- curvature: float32 [32768], P('fsdp'), may hold values from 0.001171875 to 0.01171875
- kept_counts: int32 [128], P('fsdp'), may hold values from 64 to 192, as said below
Outputs:
- curvature_product: float32 [4608, 3072], P('fsdp', 'tensor')
- normed_tangent: bfloat16 [32768, 4608], P('fsdp', 'tensor')
Inputs may be any that keep to these rules, and one draw needn't show every extreme that they name: `kept_counts`: in every draw the 2 images of some index of fsdp each keep 192 patches.
All inputs are finite; a program needn't handle non-finite values.
Results may differ from a plain program's by a relative error of at most 0.015.
Values may be sent and summed in bfloat16 or wider, within the bound.
No kernel may reach another device: no remote copies, remote signals or barrier semaphores. Data moves between devices by JAX's collectives and lax.ppermute only.
A program may use at most 128 MiB of HBM per device.

v0:
```python
import jax
import jax.numpy as jnp
from jax import lax
from jax.sharding import PartitionSpec as P

SLOTS = 256


EPS = 1e-06


def on_device(head_out, stream, tangent, norm_gain, curvature, kept_counts):
    images = kept_counts.shape[0]
    columns = stream.shape[1]
    places = jnp.arange(images * SLOTS, dtype=jnp.int32)
    slot_image = places // SLOTS
    slot_index = places % SLOTS
    image_table = slot_image[:, None] == jnp.arange(images, dtype=jnp.int32)[None, :]
    slot_counts = jnp.sum(jnp.where(image_table, kept_counts[None, :], 0), axis=1)
    live = (slot_index < slot_counts).astype(jnp.float32)
    weight = curvature * live
    partial_value = lax.dot_general(
        head_out,
        lax.all_gather(tangent, "fsdp", axis=0, tiled=True),
        (((1,), (1,)), ((), ())),
        preferred_element_type=jnp.float32,
    )
    hidden_full, gain_whole = (
        lax.all_gather(stream, "tensor", axis=1, tiled=True),
        lax.all_gather(norm_gain, "tensor", axis=0, tiled=True),
    )
    input_change = lax.psum(partial_value.astype(jnp.bfloat16), "tensor").astype(jnp.float32)
    values = hidden_full.astype(jnp.float32)
    centered_input = values - jnp.mean(values, axis=1, keepdims=True)
    inverse_scale = lax.rsqrt(
        jnp.mean(centered_input * centered_input, axis=1, keepdims=True) + EPS
    )
    standardized_input = centered_input * inverse_scale
    gain_rows = gain_whole.astype(jnp.float32)[None, :]
    normed_full = (
        gain_rows
        * (
            input_change
            - jnp.mean(input_change, axis=1, keepdims=True)
            - standardized_input
            * jnp.mean(input_change * standardized_input, axis=1, keepdims=True)
        )
        * inverse_scale
    )
    raised_output = gain_rows * weight[:, None] * normed_full
    backward_signal = (
        (
            raised_output
            - jnp.mean(raised_output, axis=1, keepdims=True)
            - standardized_input
            * jnp.mean(raised_output * standardized_input, axis=1, keepdims=True)
        )
        * inverse_scale
    ).astype(jnp.bfloat16)
    normalized_input = lax.dynamic_slice_in_dim(
        normed_full, lax.axis_index("tensor") * columns, columns, 1
    )
    product = lax.psum_scatter(
        lax.dot_general(
            backward_signal, head_out, (((0,), (0,)), ((), ())), preferred_element_type=jnp.float32
        ),
        "fsdp",
        scatter_dimension=0,
        tiled=True,
    )
    normed_slots = normalized_input * live[:, None]
    return (product, normed_slots.astype(jnp.bfloat16))


def solution(mesh):
    placed = (
        P("fsdp", "tensor"),
        P("fsdp", "tensor"),
        P("fsdp", "tensor"),
        P("tensor"),
        P("fsdp"),
        P("fsdp"),
    )
    return jax.shard_map(
        on_device,
        mesh=mesh,
        in_specs=placed,
        out_specs=(P("fsdp", "tensor"), P("fsdp", "tensor")),
        check_vma=False,
    )
```

profile of v0, /device:TPU:6, one launch (start us, length us, event | category | flops | bytes accessed | tf_op | source)
XLA Modules:
  0.0 1210.2 jit_solution(6489028261557386441)
XLA Ops:
  7.2 0.0 copy-start
  7.2 0.0 all-gather.4.cloned.1.call-start
  7.2 0.7 all-gather.4.cloned.1.call-update
  7.9 0.0 all-gather.6.cloned.1.call-start
  8.0 0.7 all-gather.6.cloned.1.call-update
  8.7 0.0 copy-start.4
  8.7 0.0 copy-start.6
  8.7 0.0 copy-start.5
  8.7 0.0 all-reduce.2.cloned.1.call-start
  8.7 147.3 %all-gather.4.cloned.1.call-done = bf16[4608,768]{1,0:T(8,128)(2,1)} async-done(((bf16[72,768]{1,0:T(8,128)(2,1)}), bf16[4608,768]{1,0:T(8,128)(2,1)}) %all-gather.4.cloned.1.call-update) | async-done | bytes 7077904 | tf_op jit(solution)/shard_map/all_gather | solution.py:24
  156.1 0.0 copy-done
  156.1 8.5 convolution_convert_fusion
  164.6 0.0 all-reduce.2.cloned.1.call-update
  164.6 0.0 reduce-scatter.2.cloned.1.call-start
  164.6 0.0 copy-done.4
  164.7 5.2 all-gather
  169.8 0.1 convert_reduce_fusion.2
  169.9 0.0 copy-done.6
  169.9 0.1 fusion.23
  170.0 0.0 copy-done.5
  170.1 38.4 %all-gather.6.cloned.1.call-done = bf16[512,4608]{1,0:T(8,128)(2,1)} async-done(((bf16[512,1152]{1,0:T(8,128)(2,1)}), bf16[512,4608]{1,0:T(8,128)(2,1)}) %all-gather.6.cloned.1.call-update) | async-done | bytes 4718608 | tf_op jit(solution)/shard_map/all_gather | solution.py:29
  208.5 3.0 convert_reduce_fusion.1
  211.5 3.7 fusion.12
  215.2 102.5 %all-reduce.2.cloned.1.call-done = bf16[512,4608]{1,0:T(8,128)(2,1)} async-done(((bf16[512,4608]{1,0:T(8,128)(2,1)}), bf16[512,4608]{1,0:T(8,128)(2,1)}) %all-reduce.2.cloned.1.call-update) | async-done | bytes 4718608 | tf_op jit(solution)/shard_map/psum | solution.py:32
  317.7 0.0 copy-start.1
  317.7 0.0 copy-start.2
  317.7 7.0 convert_reduce_fusion
  324.7 0.0 copy-done.1
  324.7 0.0 copy-done.2
  324.7 5.1 fusion.14
  329.9 0.0 copy-start.3
  329.9 3.5 copy-done.3
  333.4 9.5 fusion.15
  343.0 0.0 reduce-scatter.2.cloned.1.call-update
  343.0 2.9 multiply_convert_fusion
  345.9 857.8 %reduce-scatter.2.cloned.1.call-done = f32[72,768]{1,0:T(8,128)} async-done(((f32[4608,768]{1,0:T(8,128)}), f32[72,768]{1,0:T(8,128)}) %reduce-scatter.2.cloned.1.call-update) | async-done | bytes 221200 | tf_op jit(solution)/shard_map/reduce_scatter | solution.py:63
  (10 shorter events, 0.1 us)
Async XLA Ops:
  7.2 148.9 %copy-start = (bf16[512,768]{1,0:T(8,128)(2,1)S(1)}, bf16[512,768]{1,0:T(8,128)(2,1)}, u32[]{:S(2)}) copy-start(bf16[512,768]{1,0:T(8,128)(2,1)} %param.6) | copy-start | bytes 2359300
  7.2 148.9 %all-gather.4.cloned.1.call-start = ((), (), s32[]{:S(2)}) async-start(), calls=%async_computation.1 | async-start | bytes 7188480 | tf_op jit(solution)/shard_map/all_gather | solution.py:24
  7.9 200.5 %all-gather.6.cloned.1.call-start = ((), (), s32[]{:S(2)}) async-start(), calls=%async_computation.3 | async-start | bytes 5898240 | tf_op jit(solution)/shard_map/all_gather | solution.py:29
  8.7 156.0 %copy-start.4 = (bf16[1152]{0:T(1024)(128)(2,1)S(1)}, bf16[1152]{0:T(1024)(128)(2,1)}, u32[]{:S(2)}) copy-start(bf16[1152]{0:T(1024)(128)(2,1)} %param.9) | copy-start | bytes 6916
  8.7 161.3 %copy-start.6 = (s32[2]{0:T(128)S(1)}, s32[2]{0:T(128)}, u32[]{:S(2)}) copy-start(s32[2]{0:T(128)} %param.11) | copy-start | bytes 28
  8.7 161.4 %copy-start.5 = (f32[512]{0:T(512)S(1)}, f32[512]{0:T(512)}, u32[]{:S(2)}) copy-start(f32[512]{0:T(512)} %param.10) | copy-start | bytes 6148
  8.7 309.0 %all-reduce.2.cloned.1.call-start = ((), (), s32[]{:S(2)}) async-start(), calls=%async_computation.2 | async-start | bytes 9437184 | tf_op jit(solution)/shard_map/psum | solution.py:32
  164.6 1039.1 %reduce-scatter.2.cloned.1.call-start = ((), (), s32[]{:S(2)}) async-start(), calls=%async_computation.4 | async-start | bytes 14376960 | tf_op jit(solution)/shard_map/reduce_scatter | solution.py:63
  317.7 7.0 copy-start.1
  317.7 7.0 copy-start.2
  329.9 3.6 copy-start.3
Sparse Core Ops, SparseCore 0:
  11.7 144.3 all-gather.3
  157.9 50.5 all-gather.5
  211.1 106.5 all-reduce.1
  343.1 860.4 reduce-scatter.1
where the time goes:
time: 1210 us
  waiting for transfers between devices  1150 us (95%)
  other arithmetic  21.9 us (2%)
  matrix products  18 us (1%)
  between operations  13.9 us (1%)
    reduce_scatter x1, waiting for transfers between devices, on_device(): lax.psum_scatter(lax.dot_general(backward_signal, head_out, (((0,), (0,))...  858 us
    all_gather x1, waiting for transfers between devices, on_device(): lax.all_gather(tangent, 'fsdp', axis=0, tiled=True)  147 us
    psum x1, waiting for transfers between devices, on_device(): lax.psum(partial_value.astype(jnp.bfloat16), 'tensor').astype(jnp.float32)  103 us
    all_gather x1, waiting for transfers between devices, on_device(): lax.all_gather(stream, 'tensor', axis=1, tiled=True)  38.4 us
  transfers between devices with their start and end apart: 4, of which 4 were waited for; matrix products, arithmetic and copies ran while one was open for 2% of the time, Pallas kernels for 0%

commit v1 on v0

v1 whole, which is shorter than its diff:
```python
import jax
import jax.numpy as jnp
import numpy as np
from jax import lax
from jax.sharding import Mesh
from jax.sharding import PartitionSpec as P

SLOTS = 256
KEEP_MOST = 192
EPS = 1e-06

SIZES = {"z": 8, "h": 2, "y": 4, "l": 2, "c": 2}
ALL = tuple(SIZES)
FSDP = ("z", "h", "y")
TENSOR = ("l", "c")
ACROSS = ("h", "l", "c")


def flat(z, h, y, t):
    return ((z * 2 + h) * 4 + y) * 4 + t


TO_GROUP = [
    (flat(z, h, y, t), flat(2 * t + h, z % 2, y, z // 2))
    for z in range(8)
    for h in range(2)
    for y in range(4)
    for t in range(4)
]
FROM_GROUP = [(b, a) for a, b in TO_GROUP]
SWAP = [(0, 1), (1, 0)]


def on_device(head_out, stream, tangent, norm_gain, curvature, kept_counts):
    images = kept_counts.shape[0]
    rows = images * KEEP_MOST
    features = head_out.shape[1]
    columns = stream.shape[1]
    half = columns // 2
    width = columns * 4
    height = tangent.shape[0]
    mine = lax.axis_index("h")

    live = lax.broadcasted_iota(jnp.int32, (images, SLOTS), 1) < kept_counts[:, None]
    weight = jnp.where(live, curvature.reshape(images, SLOTS), 0.0)[:, :KEEP_MOST].reshape(rows)
    head = head_out.reshape(images, SLOTS, features)[:, :KEEP_MOST].reshape(rows, features)
    hidden = stream.reshape(images, SLOTS, columns)[:, :KEEP_MOST].reshape(rows, columns)

    block = lax.ppermute(tangent, ALL, TO_GROUP)
    heads = lax.all_gather(head, ACROSS, axis=0)
    heads = heads.reshape(2, 4, rows, features)

    def by_h(own, other):
        pair = jnp.stack([own, other])
        return jnp.where(mine == 0, pair, pair[::-1])

    own_half = lax.dynamic_slice_in_dim(hidden, mine * half, half, 1)
    other_half = lax.dynamic_slice_in_dim(hidden, (1 - mine) * half, half, 1)
    values = by_h(own_half, lax.ppermute(other_half, "h", SWAP)).reshape(2 * rows, half)
    values = values.astype(jnp.float32)
    gain = lax.dynamic_slice_in_dim(norm_gain, mine * half, half, 0).astype(jnp.float32)[None, :]
    gain2 = gain * gain

    part_mean = jnp.mean(values, axis=1)
    part_square = jnp.mean(jnp.square(values - part_mean[:, None]), axis=1)
    stats = lax.all_gather(jnp.stack([part_mean, part_square]), ACROSS, axis=0)
    weights = lax.all_gather(weight, "h", axis=0).reshape(2 * rows)
    mean = jnp.mean(stats[:, 0], axis=0)
    square = jnp.mean(stats[:, 1] + jnp.square(stats[:, 0] - mean[None]), axis=0)
    scale = lax.rsqrt(square + EPS)
    xhat = (values - mean[:, None]) * scale[:, None]

    turned = lax.all_gather(lax.all_gather(block, "y", axis=0, tiled=True), "z", axis=0, tiled=True)
    turned = turned.reshape(4, half, features)
    change = jnp.concatenate(
        [
            sum(
                lax.dot_general(
                    heads[i, a],
                    turned[a],
                    (((1,), (1,)), ((), ())),
                    preferred_element_type=jnp.float32,
                )
                for a in range(4)
            )
            for i in range(2)
        ],
        axis=0,
    )
    raised = gain2 * change
    sums = jnp.stack(
        [
            jnp.sum(change, axis=1),
            jnp.sum(change * xhat, axis=1),
            jnp.sum(raised, axis=1),
            jnp.sum(raised * xhat, axis=1),
            jnp.sum(gain2 * xhat, axis=1),
            jnp.sum(gain2 * xhat * xhat, axis=1),
            jnp.broadcast_to(jnp.sum(gain2), (2 * rows,)),
        ]
    )
    sums = jnp.sum(lax.all_gather(sums, ACROSS, axis=0), axis=0) / width
    mean_change, mean_hat, mean_up, mean_up_hat, gain_hat, gain_hat2, gain_mean = sums
    first = weights * scale * (mean_up - mean_change * gain_mean - mean_hat * gain_hat)
    second = weights * scale * (mean_up_hat - mean_change * gain_hat - mean_hat * gain_hat2)
    normed = gain * (change - mean_change[:, None] - xhat * mean_hat[:, None]) * scale[:, None]
    lifted = gain * weights[:, None] * normed
    back = (lifted - first[:, None] - xhat * second[:, None]) * scale[:, None]
    back = back.astype(jnp.bfloat16).reshape(2, rows, half)

    partial = jnp.stack(
        [
            sum(
                lax.dot_general(
                    back[i],
                    heads[i, a],
                    (((0,), (0,)), ((), ())),
                    preferred_element_type=jnp.float32,
                )
                for i in range(2)
            ).astype(jnp.bfloat16)
            for a in range(4)
        ]
    )
    partial = partial.reshape(8, 4 * height, features)
    partial = lax.psum_scatter(partial, "z", scatter_dimension=0, tiled=True)
    partial = partial.reshape(4, height, features)
    partial = lax.psum_scatter(partial, "y", scatter_dimension=0, tiled=True)
    product = lax.ppermute(partial.reshape(height, features), ALL, FROM_GROUP).astype(jnp.float32)

    normed = normed.astype(jnp.bfloat16).reshape(2, rows, half)
    kept = lax.dynamic_index_in_dim(normed, mine, 0, keepdims=False)
    sent = lax.dynamic_index_in_dim(normed, 1 - mine, 0, keepdims=False)
    both = by_h(kept, lax.ppermute(sent, "h", SWAP))
    both = jnp.concatenate([both[0], both[1]], axis=1).reshape(images, KEEP_MOST, columns)
    both = jnp.where(live[:, :KEEP_MOST, None], both, 0).astype(jnp.bfloat16)
    both = jnp.pad(both, ((0, 0), (0, SLOTS - KEEP_MOST), (0, 0)))
    return product, both.reshape(images * SLOTS, columns)


def solution(mesh):
    fine = Mesh(mesh.devices.reshape(tuple(SIZES.values())), ALL)
    placed = (
        P(FSDP, TENSOR),
        P(FSDP, TENSOR),
        P(FSDP, TENSOR),
        P(TENSOR),
        P(FSDP),
        P(FSDP),
    )
    return jax.shard_map(
        on_device,
        mesh=fine,
        in_specs=placed,
        out_specs=(P(FSDP, TENSOR), P(FSDP, TENSOR)),
        check_vma=False,
    )
```

time: 1210 us -> 269 us (0.22)
  waiting for transfers between devices: 1150 us -> 135 us
  blocking collectives: 5.19 us -> 52.7 us
  starting transfers between devices: 0.16 us -> 17.3 us
    reduce_scatter x1 -> x2, waiting for transfers between devices: 858 us -> 72.6 us  [the longest x1 48 us: on_device(): partial = lax.psum_scatter(partial, 'z', scatter_dimension=0, tiled=True)]
    all_gather x2, waiting for transfers between devices: 186 us -> 51.3 us  [the longest x1 36 us: on_device(): heads = lax.all_gather(head, ACROSS, axis=0)]
    psum x1 -> x0, waiting for transfers between devices: 103 us -> none  [on_device(): lax.psum(partial_value.astype(jnp.bfloat16), 'tensor').astype(jnp.float32)]
    all_gather x1 -> x4, blocking collectives: 5.19 us -> 52.7 us  [the longest x1 14.2 us: on_device(): sums = jnp.sum(lax.all_gather(sums, ACROSS, axis=0), axis=0) / width]
    ppermute x0 -> x4, starting transfers between devices: none -> 17.1 us  [the longest x1 8.7 us: on_device(): block = lax.ppermute(tangent, ALL, TO_GROUP)]
    reduce_sum x5 -> x8, other arithmetic: 18.9 us -> 3.86 us  [the longest x1 1.55 us: on_device(): sums = jnp.sum(lax.all_gather(sums, ACROSS, axis=0), axis=0) / width]
  transfers between devices with their start and end apart: 4 -> 8, of which waited for: 4 -> 6; matrix products, arithmetic and copies ran while one was open for 2% -> 4% of each run, Pallas kernels for 0% -> 0%
where the time goes in v1:
time: 269 us; the launch traced here: 266 us
  waiting for transfers between devices  135 us (50%)
  blocking collectives  52.7 us (20%)
  matrix products  18.8 us (7%)
  starting transfers between devices  17.3 us (6%)
  local copies, waits for them, and re-layouts  14.9 us (6%)
  between operations  14.2 us (5%)
  other arithmetic  13 us (5%)
    reduce_scatter x1, waiting for transfers between devices, on_device(): partial = lax.psum_scatter(partial, 'z', scatter_dimension=0, tiled=True)  48 us
    all_gather x1, waiting for transfers between devices, on_device(): heads = lax.all_gather(head, ACROSS, axis=0)  36 us
    reduce_scatter x1, waiting for transfers between devices, on_device(): partial = lax.psum_scatter(partial, 'y', scatter_dimension=0, tiled=True)  24.6 us
    all_gather x1, waiting for transfers between devices, on_device(): lax.all_gather(lax.all_gather(block, 'y', axis=0, tiled=True), 'z', axis=...  15.3 us
    all_gather x1, blocking collectives, on_device(): sums = jnp.sum(lax.all_gather(sums, ACROSS, axis=0), axis=0) / width  14.2 us
    all_gather x1, blocking collectives, on_device(): lax.all_gather(block, 'y', axis=0, tiled=True)  13.9 us
    all_gather x1, blocking collectives, on_device(): stats = lax.all_gather(jnp.stack([part_mean, part_square]), ACROSS, axis=0)  12.8 us
    all_gather x1, blocking collectives, on_device(): weights = lax.all_gather(weight, 'h', axis=0).reshape(2 * rows)  11.8 us
  transfers between devices with their start and end apart: 8, of which 6 were waited for; matrix products, arithmetic and copies ran while one was open for 4% of the time, Pallas kernels for 0%

profile of v1, /device:TPU:6, one launch (start us, length us, event | category | flops | bytes accessed | tf_op | source)
XLA Modules:
  0.0 266.4 jit_solution(12675372335482757333)
XLA Ops:
  7.2 8.7 %collective-permute-start = (bf16[72,768]{1,0:T(8,128)(2,1)}, bf16[72,768]{1,0:T(8,128)(2,1)S(1)}, u32[]{:S(2)}, u32[]{:S(2)}) collective-permute-start(bf16[72,768]{1,0:T(8,128)(2,1)} %param.8), channel_id=1, source_target_pairs={{0,0},{1,64},{2,128},{3,192},{4,4},{5,68},{6,132},{7,196},{8,8},{9... | collective-permute-start | bytes 331784 | tf_op jit(solution)/shard_map/ppermute | solution.py:49
  15.9 7.1 %collective-permute-done = bf16[72,768]{1,0:T(8,128)(2,1)S(1)} collective-permute-done((bf16[72,768]{1,0:T(8,128)(2,1)}, bf16[72,768]{1,0:T(8,128)(2,1)S(1)}, u32[]{:S(2)}, u32[]{:S(2)}) %collective-permute-start) | collective-permute-done | bytes 110624 | tf_op jit(solution)/shard_map/ppermute | solution.py:49
  23.0 13.9 %all_gather.26 = bf16[288,768]{1,0:T(8,128)(2,1)} all-gather(bf16[72,768]{1,0:T(8,128)(2,1)S(1)} %collective-permute-done), channel_id=1, replica_groups=mesh['z'=8,'h'=2,'y'=4,'l'=2,'c'=2] {'y'}, dimensions={0}, use_global_device_ids=true | all-gather | bytes 552960 | tf_op jit(solution)/shard_map/all_gather | solution.py:73
  37.0 1.9 slice.115
  39.1 0.4 constant_dynamic-slice_fusion.2
  39.8 0.5 copy-done.10
  40.4 11.8 %all-gather.2 = f32[2,1,384]{2,1,0:T(1,128)S(1)} all-gather(f32[1,1,384]{2,1,0:T(1,128)S(1)} %reshape.287), channel_id=1, replica_groups=mesh['z'=8,'h'=2,'y'=4,'l'=2,'c'=2] {'h'}, dimensions={0}, use_global_device_ids=true | all-gather | bytes 4608 | tf_op jit(solution)/shard_map/all_gather | solution.py:67
  52.2 0.6 mul.189
  52.8 0.2 copy.21
  53.1 0.7 dynamic-slice_convert_fusion
  53.7 0.7 fusion.51
  54.4 0.2 copy.22
  54.8 0.2 convert_reduce_fusion
  55.0 0.3 fusion.2
  55.3 12.8 %all-gather.3 = f32[8,2,768]{2,1,0:T(2,128)S(1)} all-gather(f32[1,2,768]{2,1,0:T(2,128)S(1)} %maximum_bitcast_fusion), channel_id=2, replica_groups=mesh['z'=8,'h'=2,'y'=4,'l'=2,'c'=2] {'h','l','c'}, dimensions={0}, use_global_device_ids=true | all-gather | bytes 55296 | tf_op jit(solution)/shard_map/all_gather | solution.py:66
  68.2 0.6 div.29
  68.8 0.6 rsqrt.18
  69.5 1.4 copy.33
  71.0 15.3 %all-gather.10.cloned.1.call-done = bf16[2304,768]{1,0:T(8,128)(2,1)} async-done(((bf16[288,768]{1,0:T(8,128)(2,1)}), bf16[2304,768]{1,0:T(8,128)(2,1)}) %all-gather.10.cloned.1.call-update) | async-done | bytes 3538960 | tf_op jit(solution)/shard_map/all_gather | solution.py:73
  86.3 36.0 %all-gather.8.cloned.1.call-done = bf16[8,384,768]{2,1,0:T(8,128)(2,1)} async-done(((bf16[1,384,768]{2,1,0:T(8,128)(2,1)}), bf16[8,384,768]{2,1,0:T(8,128)(2,1)}) %all-gather.8.cloned.1.call-update) | async-done | bytes 4718608 | tf_op jit(solution)/shard_map/all_gather | solution.py:50
  122.3 2.1 fusion.21
  124.4 2.0 fusion.25
  126.4 2.0 fusion.29
  128.4 1.8 fusion.23
  130.2 0.6 fusion.27
  130.9 0.6 fusion.31
  131.5 0.7 fusion.16
  132.2 0.7 fusion.14
  132.9 0.3 multiply_reduce_fusion.1
  133.2 0.6 copy-done
  133.8 0.6 stack.63
  134.4 0.6 stack.57
  135.0 0.8 fusion
  135.8 0.6 copy.36
  136.4 0.6 copy.37
  137.0 1.2 stack_broadcast_in_dim.3
  138.2 1.3 stack.67
  139.5 14.2 %all-gather.4 = f32[8,7,768]{2,1,0:T(8,128)} all-gather(f32[1,7,768]{2,1,0:T(8,128)} %bitcast.137), channel_id=3, replica_groups=mesh['z'=8,'h'=2,'y'=4,'l'=2,'c'=2] {'h','l','c'}, dimensions={0}, use_global_device_ids=true | all-gather | bytes 193536 | tf_op jit(solution)/shard_map/all_gather | solution.py:102
  153.8 1.6 reduce_sum.119
  155.3 0.7 broadcast_multiply_fusion
  156.1 0.7 subtract_multiply_fusion.1
  156.8 2.7 %multiply_convert_fusion = bf16[768,576]{0,1:T(8,128)(2,1)S(1)} fusion(f32[768,576]{0,1:T(8,128)} %bitcast.125, f32[768]{0:T(1024)S(1)} %get-tuple-element.28, f32[768]{0:T(1024)S(1)} %get-tuple-element.27, f32[768]{0:T(1024)S(1)} %get-tuple-element.15, f32[768]{0:T(1024)} %copy-done.4, f32[768]{0:T(1024)S(1)} %broadcast_multiply_fusion.1, ...), kind=kLoop, calls=%fused_computation.27 | loop fusion | flops 6635520 | bytes 4447488 | tf_op jit(solution)/shard_map/convert_element_type | solution.py:109
  159.5 1.7 fusion.36
  161.3 1.7 fusion.37
  162.9 1.7 fusion.38
  164.7 0.6 fusion.35
  165.3 0.6 fusion.18
  165.9 0.6 fusion.19
  166.5 0.6 fusion.20
  167.2 0.6 fusion.17
  167.8 2.0 pad_maximum_fusion
  170.0 0.6 copy-done.5
  170.6 0.6 fusion.12
  171.2 1.5 collective-permute-start.3
  172.8 48.0 %reduce-scatter.3.cloned.1.call-done = bf16[1,288,768]{2,1,0:T(8,128)(2,1)} async-done(((bf16[8,288,768]{2,1,0:T(8,128)(2,1)}), bf16[1,288,768]{2,1,0:T(8,128)(2,1)}) %reduce-scatter.3.cloned.1.call-update) | async-done | bytes 442384 | tf_op jit(solution)/shard_map/reduce_scatter | solution.py:126
  220.9 0.2 reverse_select_fusion
  221.2 0.3 copy.28
  221.5 0.3 copy.29
  221.7 24.6 %reduce-scatter.5.cloned.1.call-done = bf16[1,72,768]{2,1,0:T(8,128)(2,1)} async-done(((bf16[4,72,768]{2,1,0:T(8,128)(2,1)}), bf16[1,72,768]{2,1,0:T(8,128)(2,1)}) %reduce-scatter.5.cloned.1.call-update) | async-done | bytes 110608 | tf_op jit(solution)/shard_map/reduce_scatter | solution.py:128
  246.3 6.8 %collective-permute-start.2 = (bf16[72,768]{1,0:T(8,128)(2,1)}, bf16[72,768]{1,0:T(8,128)(2,1)S(1)}, u32[]{:S(2)}, u32[]{:S(2)}) collective-permute-start(bf16[72,768]{1,0:T(8,128)(2,1)} %bitcast.149), channel_id=1, source_target_pairs={{0,0},{64,1},{128,2},{192,3},{4,4},{68,5},{132,6},{196,7},{8,8},{7... | collective-permute-start | bytes 331784 | tf_op jit(solution)/shard_map/ppermute | solution.py:129
  253.2 0.5 maximum_select_fusion
  253.7 1.1 pad.4
  254.8 4.4 %collective-permute-done.2 = bf16[72,768]{1,0:T(8,128)(2,1)S(1)} collective-permute-done((bf16[72,768]{1,0:T(8,128)(2,1)}, bf16[72,768]{1,0:T(8,128)(2,1)S(1)}, u32[]{:S(2)}, u32[]{:S(2)}) %collective-permute-start.2) | collective-permute-done | bytes 110624 | tf_op jit(solution)/shard_map/ppermute | solution.py:129
  259.1 0.7 convert_element_type.53
  (68 shorter events, 1.4 us)
Async XLA Ops:
  7.2 31.8 %copy-start.3 = (bf16[512,1152]{1,0:T(8,128)(2,1)S(1)}, bf16[512,1152]{1,0:T(8,128)(2,1)}, u32[]{:S(2)}) copy-start(bf16[512,1152]{1,0:T(8,128)(2,1)} %param.7) | copy-start | bytes 3538948
  7.2 79.1 %all-gather.10.cloned.1.call-start = ((), (), s32[]{:S(2)}) async-start(), calls=%async_computation.3 | async-start | bytes 3981312 | tf_op jit(solution)/shard_map/all_gather | solution.py:73
  7.2 15.8 %collective-permute-start = (bf16[72,768]{1,0:T(8,128)(2,1)}, bf16[72,768]{1,0:T(8,128)(2,1)S(1)}, u32[]{:S(2)}, u32[]{:S(2)}) collective-permute-start(bf16[72,768]{1,0:T(8,128)(2,1)} %param.8), channel_id=1, source_target_pairs={{0,0},{1,64},{2,128},{3,192},{4,4},{5,68},{6,132},{7,196},{8,8},{9... | collective-permute-start | bytes 331784 | tf_op jit(solution)/shard_map/ppermute | solution.py:49
  36.9 85.4 %all-gather.8.cloned.1.call-start = ((), (), s32[]{:S(2)}) async-start(), calls=%async_computation.2 | async-start | bytes 5308416 | tf_op jit(solution)/shard_map/all_gather | solution.py:50
  38.9 181.9 %reduce-scatter.3.cloned.1.call-start = ((), (), s32[]{:S(2)}) async-start(), calls=%async_computation.4 | async-start | bytes 3981312 | tf_op jit(solution)/shard_map/reduce_scatter | solution.py:126
  39.0 0.7 copy-start.13
  39.0 0.7 copy-start.14
  39.1 14.0 %copy-start.12 = (bf16[1152]{0:T(1024)(128)(2,1)S(1)}, bf16[1152]{0:T(1024)(128)(2,1)}, u32[]{:S(2)}) copy-start(bf16[1152]{0:T(1024)(128)(2,1)} %param.9) | copy-start | bytes 6916
  39.6 14.9 %collective-permute-start.1 = (bf16[384,576]{1,0:T(8,128)(2,1)S(1)}, bf16[384,576]{1,0:T(8,128)(2,1)S(1)}, u32[]{:S(2)}, u32[]{:S(2)}) collective-permute-start(bf16[384,576]{1,0:T(8,128)(2,1)S(1)} %get-tuple-element.23), channel_id=1, source_target_pairs={{0,16},{16,0},{1,17},{17,1},{2,18},{18,2},{3,19},{19,3},{4,20},{20... | collective-permute-start | bytes 1327112 | tf_op jit(solution)/shard_map/ppermute | solution.py:59
  39.8 0.5 copy-start.10
  68.8 2.2 copy-start.4
  122.3 4.1 %copy-start.1 = (bf16[8,384,768]{2,1,0:T(8,128)(2,1)S(1)}, bf16[8,384,768]{2,1,0:T(8,128)(2,1)}, u32[]{:S(2)}) copy-start(bf16[8,384,768]{2,1,0:T(8,128)(2,1)} %all-gather.8.cloned.1.call-done) | copy-start | bytes 14155780
  126.4 3.8 %copy-start.2 = (bf16[2304,768]{1,0:T(8,128)(2,1)S(1)}, bf16[2304,768]{1,0:T(8,128)(2,1)}, u32[]{:S(2)}) copy-start(bf16[2304,768]{1,0:T(8,128)(2,1)} %all-gather.10.cloned.1.call-done) | copy-start | bytes 10616836
  132.9 0.9 copy-start
  132.9 2.1 copy-start.6
  132.9 2.1 copy-start.8
  156.8 7.8 %slice-start = ((s8[4718592]{0:T(1024)(128)(4,1)}), s8[4194304]{0:T(1024)(128)(4,1)S(1)}, s32[]{:S(2)}) async-start(s8[4718592]{0:T(1024)(128)(4,1)} %bitcast.118), calls=%async_computation.6 | async-start | bytes 8388608
  159.5 5.1 %slice-start.1 = ((s8[4718592]{0:T(1024)(128)(4,1)}), s8[524288]{0:T(1024)(128)(4,1)S(1)}, s32[]{:S(2)}) async-start(s8[4718592]{0:T(1024)(128)(4,1)} %bitcast.118), calls=%async_computation.7 | async-start | bytes 1048576
  169.9 0.7 copy-start.5
  169.9 0.7 copy-start.7
  169.9 0.7 copy-start.9
  169.9 76.5 %reduce-scatter.5.cloned.1.call-start = ((), (), s32[]{:S(2)}) async-start(), calls=%async_computation.5 | async-start | bytes 552960 | tf_op jit(solution)/shard_map/reduce_scatter | solution.py:128
  171.2 49.6 %collective-permute-start.3 = (bf16[384,576]{0,1:T(8,128)(2,1)S(1)}, bf16[384,576]{0,1:T(8,128)(2,1)S(1)}, u32[]{:S(2)}, u32[]{:S(2)}) collective-permute-start(bf16[384,576]{0,1:T(8,128)(2,1)S(1)} %get-tuple-element.21), channel_id=1, source_target_pairs={{0,16},{16,0},{1,17},{17,1},{2,18},{18,2},{3,19},{19,3},{4,20},{20... | collective-permute-start | bytes 1327112 | tf_op jit(solution)/shard_map/ppermute | solution.py:134
  221.1 32.1 %copy-start.11 = (pred[2,256]{1,0:T(4,128)(4,1)S(1)}, pred[2,256]{1,0:T(4,128)(4,1)}, u32[]{:S(2)}) copy-start(pred[2,256]{1,0:T(4,128)(4,1)} %copy-done.10) | copy-start | bytes 1540
  246.3 12.8 %collective-permute-start.2 = (bf16[72,768]{1,0:T(8,128)(2,1)}, bf16[72,768]{1,0:T(8,128)(2,1)S(1)}, u32[]{:S(2)}, u32[]{:S(2)}) collective-permute-start(bf16[72,768]{1,0:T(8,128)(2,1)} %bitcast.149), channel_id=1, source_target_pairs={{0,0},{64,1},{128,2},{192,3},{4,4},{68,5},{132,6},{196,7},{8,8},{7... | collective-permute-start | bytes 331784 | tf_op jit(solution)/shard_map/ppermute | solution.py:129
Sparse Core Ops, SparseCore 0:
  37.0 49.1 all-gather.9
  88.7 33.5 all-gather.7
  170.0 50.7 reduce-scatter.2
  223.4 22.9 reduce-scatter.4
